TPU v7x, 32 devices: a whole 2x2x4 slice. The times are simulated.
32 devices in a mesh: rows: 8 (over z, x), tp: 4 (over y, core).
Axes of the slice: x: 2, y: 2, z: 4, core: 2. Of those that a mesh axis runs over, the one named last changes fastest.
Arguments:
- hidden: bfloat16 [256, 1024], P(('rows', 'tp')), may hold values from -6 to 6
- context: bfloat16 [256, 1024], P(('rows', 'tp')), may hold values from -4 to 4
- byte_input_codes: int32 [256, 4], P(('rows', 'tp')), may hold values from 0 to 255
- finish: int32 [256, 4], P('rows'), may hold values from 0 to 1, as said below
- cache_len: int32 [256], P('rows'), may hold values from 1 to 256, as said below
- embed: bfloat16 [256, 1024], replicated, may hold values from -6 to 6
- gain_local: float32 [1024], replicated, may hold values from 0.1 to 1.9
- w_in: bfloat16 [1024, 2048], replicated, may hold values from -0.1875 to 0.1875
- w_out: bfloat16 [2048, 1024], replicated, may hold values from -0.125 to 0.125
- output_norm_gain: float32 [1024], replicated, may hold values from 0.25 to 1.75
- w_vocab: bfloat16 [1024, 256], replicated, may hold values from -0.1875 to 0.1875
- w_up: bfloat16 [1024, 8192], P(None, 'rows')
- gain_global: bfloat16 [8192], P('rows'), may hold values from 0.099609375 to 1.8984375
- w_query: bfloat16 [8192, 8192], P('rows', 'tp'), may hold values from -0.0625 to 0.0625
- w_key: bfloat16 [8192, 1024], P('rows', 'tp'), may hold values from -0.0625 to 0.0625
- w_value: bfloat16 [8192, 1024], P('rows', 'tp'), may hold values from -0.0625 to 0.0625
- key_cache: bfloat16 [256, 256, 1024], P('rows', None, 'tp')
- value_cache: bfloat16 [256, 256, 1024], P('rows', None, 'tp'), may hold values from -6 to 6
- w_mix: bfloat16 [8192, 1024], P('tp'), may hold values from -0.0625 to 0.0625
Outputs:
- logits: float32 [256, 4, 256], P(('rows', 'tp'))
- context_out: bfloat16 [256, 1024], P(('rows', 'tp'))
Inputs may be any that keep to these rules, and one draw needn't show every extreme that they name: Of the 8 rows of one block at one step at most 5 have finish 1; in every draw some step has 5 of them in each of the blocks that share one index of rows. `cache_len`: some row has 256.
All inputs are finite; a program needn't handle non-finite values.
Results may differ from a plain program's by a relative error of at most 0.039.
Values may be sent and summed in bfloat16 or wider, within the bound.
A program may use at most 192 MiB of HBM per device.

v0:
```python
import jax
import jax.numpy as jnp
from jax import lax
from jax.sharding import PartitionSpec as P

DG = 8192
HEADS = 64
KVH = 8
HD = 128
STEPS = 4
CAP = 5


EPS = 1e-05


def rms_scale(values, gain):
    mean_sq = jnp.mean(values * values, axis=-1, keepdims=True)
    return values * lax.rsqrt(mean_sq + EPS) * gain


def slot_picker(finished, capacity):
    ranked = jnp.cumsum(finished, axis=-1) - 1
    slot_ids = jnp.arange(capacity, dtype=jnp.int32)
    chosen = (finished[..., None, :] == 1) & (ranked[..., None, :] == slot_ids[:, None])
    return chosen.astype(jnp.int32)


def attend(query_rows, fresh_key_rows, new_values, keys, values, lengths):
    head_size = query_rows.shape[-1]
    logit_scale = 1.0 / jnp.sqrt(jnp.float32(head_size))
    scores = (
        jnp.einsum("bkgd,btkd->bkgt", query_rows, keys, preferred_element_type=jnp.float32)
        * logit_scale
    )
    positions = jnp.arange(keys.shape[1], dtype=jnp.int32)
    valid = positions[None, :] < lengths[:, None]
    scores = jnp.where(valid[:, None, None, :], scores, -jnp.inf)
    self_token = (
        jnp.einsum("orey,ory->ore", query_rows, fresh_key_rows, preferred_element_type=jnp.float32)
        * logit_scale
    )
    top = jnp.maximum(jnp.max(scores, axis=-1), self_token)
    weights = jnp.exp(scores - top[..., None])
    own_weight = jnp.exp(self_token - top)
    total = jnp.sum(weights, axis=-1) + own_weight
    probs = (weights / total[..., None]).astype(jnp.bfloat16)
    own_prob = (own_weight / total).astype(jnp.bfloat16)
    mixed = jnp.einsum("bkgt,btkd->bkgd", probs, values, preferred_element_type=jnp.float32)
    mixed = (
        mixed
        + own_prob.astype(jnp.float32)[..., None] * new_values.astype(jnp.float32)[:, :, None, :]
    )
    return mixed.astype(jnp.bfloat16).reshape(query_rows.shape[0], -1)


def on_device(
    hidden,
    context,
    byte_input_codes,
    finish,
    cache_len,
    embed,
    gain_local,
    w_in,
    w_out,
    output_norm_gain,
    w_vocab,
    w_up,
    gain_global,
    w_query,
    w_key,
    w_value,
    key_cache,
    value_cache,
    w_mix,
):
    n_tp = lax.axis_size("tp")
    tp_index = lax.axis_index("tp")
    rows_index = lax.axis_index("rows")
    row_count = hidden.shape[0]
    capacity = CAP
    block_slots = n_tp * capacity
    head_group = HEADS // KVH
    query_cols = w_query.shape[1]
    kv_cols = w_key.shape[1]
    kv_local = kv_cols // HD
    cache_size = key_cache.shape[1]
    vocab_size = embed.shape[0]
    finish_mine = lax.dynamic_slice_in_dim(finish, tp_index * row_count, row_count, 0)
    w_qkv = jnp.concatenate([w_query, w_key, w_value], axis=1)
    state = hidden.astype(jnp.float32)
    ctx = context
    logit_list = []
    for byte_step in range(STEPS):
        one_hot = (
            byte_input_codes[:, byte_step][:, None]
            == jnp.arange(vocab_size, dtype=jnp.int32)[None, :]
        ).astype(jnp.bfloat16)
        embedded = jnp.dot(one_hot, embed, preferred_element_type=jnp.float32)
        x_val = state + embedded + ctx.astype(jnp.float32)
        normed_loc = rms_scale(x_val, gain_local).astype(jnp.bfloat16)
        inner = jax.nn.silu(jnp.dot(normed_loc, w_in, preferred_element_type=jnp.float32)).astype(
            jnp.bfloat16
        )
        state = x_val + jnp.dot(inner, w_out, preferred_element_type=jnp.float32)
        final = rms_scale(state, output_norm_gain).astype(jnp.bfloat16)
        logit_list.append(jnp.dot(final, w_vocab, preferred_element_type=jnp.float32))
        my_finished = finish_mine[:, byte_step]
        my_picker = slot_picker(my_finished, capacity).astype(jnp.bfloat16)
        slot_h = jnp.dot(
            my_picker, state.astype(jnp.bfloat16), preferred_element_type=jnp.float32
        ).astype(jnp.bfloat16)
        all_slots = lax.all_gather(slot_h, ("rows", "tp"), axis=0, tiled=True)
        upper = jnp.dot(all_slots, w_up, preferred_element_type=jnp.float32)
        sq_total = lax.psum(jnp.sum(upper * upper, axis=1), "rows")
        normed = (upper * gain_global.astype(jnp.float32)).astype(jnp.bfloat16)
        qkv = lax.psum_scatter(
            jnp.dot(normed, w_qkv, preferred_element_type=jnp.float32),
            "rows",
            scatter_dimension=0,
            tiled=True,
        )
        sq_block = lax.dynamic_slice_in_dim(sq_total, rows_index * block_slots, block_slots, 0)
        inv = lax.rsqrt(sq_block / DG + EPS)[:, None]
        qkv = (qkv * inv).astype(jnp.bfloat16)
        query = qkv[:, :query_cols].reshape(block_slots, kv_local, head_group, HD)
        new_key = qkv[:, query_cols : query_cols + kv_cols].reshape(block_slots, kv_local, HD)
        new_value = qkv[:, query_cols + kv_cols :].reshape(block_slots, kv_local, HD)
        group_finished = finish[:, byte_step].reshape(n_tp, row_count)
        group_picker = slot_picker(group_finished, capacity)
        local_row = jnp.sum(group_picker * jnp.arange(row_count, dtype=jnp.int32), axis=-1)
        row_index = (local_row + jnp.arange(n_tp, dtype=jnp.int32)[:, None] * row_count).reshape(
            block_slots
        )
        keys = jnp.take(key_cache, row_index, axis=0).reshape(block_slots, cache_size, kv_local, HD)
        values = jnp.take(value_cache, row_index, axis=0).reshape(
            block_slots, cache_size, kv_local, HD
        )
        lengths = jnp.take(cache_len, row_index, axis=0)
        attended = attend(query, new_key, new_value, keys, values, lengths)
        patch_context_state = lax.psum_scatter(
            jnp.dot(attended, w_mix, preferred_element_type=jnp.float32),
            "tp",
            scatter_dimension=0,
            tiled=True,
        ).astype(jnp.bfloat16)
        delivered = jnp.dot(
            my_picker.T, patch_context_state, preferred_element_type=jnp.float32
        ).astype(jnp.bfloat16)
        ctx = jnp.where((my_finished == 1)[:, None], delivered, ctx)
    return (jnp.stack(logit_list, axis=1), ctx)


def solution(mesh):
    in_specs = (
        P(("rows", "tp"), None),
        P(("rows", "tp"), None),
        P(("rows", "tp"), None),
        P("rows", None),
        P("rows"),
        P(),
        P(),
        P(),
        P(),
        P(),
        P(),
        P(None, "rows"),
        P("rows"),
        P("rows", "tp"),
        P("rows", "tp"),
        P("rows", "tp"),
        P("rows", None, "tp"),
        P("rows", None, "tp"),
        P("tp", None),
    )
    out_specs = (P(("rows", "tp"), None, None), P(("rows", "tp"), None))
    return jax.shard_map(
        on_device, mesh=mesh, in_specs=in_specs, out_specs=out_specs, check_vma=False
    )
```

profile of v0, /device:TPU:11, one launch (start us, length us, event | category | flops | bytes accessed | tf_op | source)
XLA Modules:
  0.0 661.9 jit_solution(12191213578414125104)
XLA Ops:
  2.8 4.8 constant_dynamic-update-slice_fusion.2
  8.8 4.8 multiply_reduce_fusion.10
  13.7 33.7 %all-gather = bf16[32,5,1024]{2,1,0:T(8,128)(2,1)S(1)} all-gather(bf16[1,5,1024]{2,1,0:T(8,128)(2,1)S(1)} %fusion.96), channel_id=1, replica_groups=mesh['rows'=8,'tp'=4] {'rows','tp'}, dimensions={0}, use_global_device_ids=true | all-gather | bytes 337920 | tf_op jit(solution)/shard_map/all_gather | solution.py:114
  49.5 1.9 constant_dynamic-update-slice_fusion
  52.0 4.8 fusion.104
  56.8 43.7 %fusion = f32[24,2560]{1,0:T(8,128)S(1)} fusion(f32[160,2560]{1,0:T(8,128)} %fusion.104), kind=kCustom, calls=%all-reduce-scatter | all-reduce-scatter fusion | flops 491521 | bytes 1884672
  100.5 6.1 collective-permute-start
  106.6 3.2 collective-permute-start.1
  111.7 4.5 gather_fusion.1
  117.1 4.5 gather_fusion.4
  122.3 4.6 gather_fusion.2
  127.0 4.5 gather_fusion.5
  131.7 4.6 gather_fusion.7
  136.9 4.5 gather_fusion.8
  141.7 4.6 gather_fusion.10
  147.0 4.6 gather_fusion.11
  151.6 16.8 %psum.28 = f32[160]{0:T(256)S(1)} all-reduce(f32[160]{0:T(256)S(1)} %get-tuple-element.66), channel_id=1, replica_groups=mesh['rows'=8,'tp'=4] {'rows'}, use_global_device_ids=true, to_apply=%region_7.9 | all-reduce | flops 160 | bytes 1280 | tf_op jit(solution)/shard_map/psum | solution.py:116
  171.7 5.5 select_bitcast_fusion.7
  177.2 3.2 select_bitcast_fusion.5
  181.6 3.2 select_bitcast_fusion.3
  186.0 2.9 select_bitcast_fusion.1
  191.6 2.1 concatenate.4
  194.0 2.6 fusion.225
  197.0 2.4 fusion.80
  200.6 11.6 %fusion.1 = f32[8,1024]{1,0:T(8,128)S(1)} fusion(f32[20,1024]{1,0:T(8,128)S(1)} %fusion.229), kind=kCustom, calls=%all-reduce-scatter.1 | all-reduce-scatter fusion | flops 32769 | bytes 115200
  212.3 2.0 collective-permute-start.3
  214.3 1.9 collective-permute-start.2
  219.2 5.3 multiply_reduce_fusion.8
  224.6 36.2 %all-gather.1 = bf16[32,5,1024]{2,1,0:T(8,128)(2,1)} all-gather(bf16[1,5,1024]{2,1,0:T(8,128)(2,1)S(1)} %fusion.98), channel_id=1, replica_groups=mesh['rows'=8,'tp'=4] {'rows','tp'}, dimensions={0}, use_global_device_ids=true | all-gather | bytes 337920 | tf_op jit(solution)/shard_map/all_gather | solution.py:114
  262.7 4.8 fusion.105
  267.4 43.7 %fusion.2 = f32[24,2560]{1,0:T(8,128)S(1)} fusion(f32[160,2560]{1,0:T(8,128)} %fusion.105), kind=kCustom, calls=%all-reduce-scatter.2 | all-reduce-scatter fusion | flops 491521 | bytes 1884672
  311.2 6.3 collective-permute-start.4
  317.4 3.1 collective-permute-start.5
  320.5 14.5 %psum.29 = f32[160]{0:T(256)S(1)} all-reduce(f32[160]{0:T(256)S(1)} %get-tuple-element.72), channel_id=1, replica_groups=mesh['rows'=8,'tp'=4] {'rows'}, use_global_device_ids=true, to_apply=%region_18.21 | all-reduce | flops 160 | bytes 1280 | tf_op jit(solution)/shard_map/psum | solution.py:116
  335.6 4.1 concatenate.6
  342.0 2.6 fusion.226
  346.9 2.5 fusion.83
  350.6 12.8 %fusion.3 = f32[8,1024]{1,0:T(8,128)S(1)} fusion(f32[20,1024]{1,0:T(8,128)S(1)} %fusion.230), kind=kCustom, calls=%all-reduce-scatter.3 | all-reduce-scatter fusion | flops 32769 | bytes 115200
  365.2 3.8 collective-permute-start.6
  370.7 5.3 multiply_reduce_fusion.6
  376.2 37.3 %all-gather.2 = bf16[32,5,1024]{2,1,0:T(8,128)(2,1)} all-gather(bf16[1,5,1024]{2,1,0:T(8,128)(2,1)S(1)} %fusion.100), channel_id=1, replica_groups=mesh['rows'=8,'tp'=4] {'rows','tp'}, dimensions={0}, use_global_device_ids=true | all-gather | bytes 337920 | tf_op jit(solution)/shard_map/all_gather | solution.py:114
  415.3 4.7 fusion.106
  420.0 43.7 %fusion.4 = f32[24,2560]{1,0:T(8,128)S(1)} fusion(f32[160,2560]{1,0:T(8,128)} %fusion.106), kind=kCustom, calls=%all-reduce-scatter.4 | all-reduce-scatter fusion | flops 491521 | bytes 1884672
  463.7 6.3 collective-permute-start.8
  470.0 3.1 collective-permute-start.9
  473.1 14.4 %psum.30 = f32[160]{0:T(256)S(1)} all-reduce(f32[160]{0:T(256)S(1)} %get-tuple-element.78), channel_id=1, replica_groups=mesh['rows'=8,'tp'=4] {'rows'}, use_global_device_ids=true, to_apply=%region_29.32 | all-reduce | flops 160 | bytes 1280 | tf_op jit(solution)/shard_map/psum | solution.py:116
  488.1 4.1 concatenate.8
  494.5 2.6 fusion.227
  499.4 2.5 fusion.86
  503.1 12.5 %fusion.5 = f32[8,1024]{1,0:T(8,128)S(1)} fusion(f32[20,1024]{1,0:T(8,128)S(1)} %fusion.231), kind=kCustom, calls=%all-reduce-scatter.5 | all-reduce-scatter fusion | flops 32769 | bytes 115200
  515.7 2.0 collective-permute-start.11
  517.8 1.9 collective-permute-start.10
  521.7 4.8 multiply_reduce_fusion.4
  526.6 34.6 %all-gather.3 = bf16[32,5,1024]{2,1,0:T(8,128)(2,1)S(1)} all-gather(bf16[1,5,1024]{2,1,0:T(8,128)(2,1)S(1)} %fusion.102), channel_id=1, replica_groups=mesh['rows'=8,'tp'=4] {'rows','tp'}, dimensions={0}, use_global_device_ids=true | all-gather | bytes 337920 | tf_op jit(solution)/shard_map/all_gather | solution.py:114
  562.0 4.7 fusion.107
  566.7 43.8 %fusion.6 = f32[24,2560]{1,0:T(8,128)S(1)} fusion(f32[160,2560]{1,0:T(8,128)} %fusion.107), kind=kCustom, calls=%all-reduce-scatter.6 | all-reduce-scatter fusion | flops 491521 | bytes 1884672
  610.6 6.3 collective-permute-start.12
  616.9 3.1 collective-permute-start.13
  620.0 14.6 %psum.31 = f32[160]{0:T(256)S(1)} all-reduce(f32[160]{0:T(256)S(1)} %get-tuple-element.92), channel_id=1, replica_groups=mesh['rows'=8,'tp'=4] {'rows'}, use_global_device_ids=true, to_apply=%region_40.43 | all-reduce | flops 160 | bytes 1280 | tf_op jit(solution)/shard_map/psum | solution.py:116
  636.6 2.6 fusion.228
  639.5 2.4 fusion.89
  643.1 12.5 %fusion.7 = f32[8,1024]{1,0:T(8,128)S(1)} fusion(f32[20,1024]{1,0:T(8,128)S(1)} %fusion.232), kind=kCustom, calls=%all-reduce-scatter.7 | all-reduce-scatter fusion | flops 32769 | bytes 115200
  655.7 2.0 collective-permute-start.15
  657.7 1.9 collective-permute-start.14
  (303 shorter events, 51.4 us)
Async XLA Ops:
  0.6 50.8 %copy-start = (bf16[1024,1024]{1,0:T(8,128)(2,1)S(1)}, bf16[1024,1024]{1,0:T(8,128)(2,1)}, u32[]{:S(2)}) copy-start(bf16[1024,1024]{1,0:T(8,128)(2,1)} %param.34) | copy-start | bytes 6291460
  2.7 10.9 %copy-start.33 = (pred[8]{0:T(512)(128)(4,1)}, pred[8]{0:T(512)(128)(4,1)S(1)}, u32[]{:S(2)}) copy-start(pred[8]{0:T(512)(128)(4,1)S(1)} %get-tuple-element.41) | copy-start | bytes 28
  2.7 4.9 copy-start.47
  2.7 5.5 copy-start.12
  2.7 5.5 copy-start.19
  2.7 5.5 copy-start.27
  2.8 6.0 copy-start.18
  8.8 4.8 copy-start.39
  8.8 38.8 %copy-start.46 = (bf16[1024]{0:T(1024)(128)(2,1)S(1)}, bf16[1024]{0:T(1024)(128)(2,1)}, u32[]{:S(2)}) copy-start(bf16[1024]{0:T(1024)(128)(2,1)} %param.35) | copy-start | bytes 6148
  52.0 57.8 %copy-start.28 = (s32[32,4]{0,1:T(4,128)S(1)}, s32[32,4]{0,1:T(4,128)}, u32[]{:S(2)}) copy-start(s32[32,4]{0,1:T(4,128)} %param.26) | copy-start | bytes 1540
  100.5 91.1 %collective-permute-start = (f32[24,2560]{1,0:T(8,128)S(1)}, f32[24,2560]{1,0:T(8,128)}, u32[]{:S(2)}, u32[]{:S(2)}) collective-permute-start(f32[24,2560]{1,0:T(8,128)S(1)} %fusion), channel_id=1, source_target_pairs={{0,4},{4,8},{8,12},{12,16},{16,20},{20,24},{24,28},{1,5},{5,9},{9,... | collective-permute-start | bytes 737288
  106.6 84.4 %collective-permute-start.1 = (f32[4,2560]{1,0:T(4,128)S(1)}, f32[4,2560]{1,0:T(4,128)S(1)}, u32[]{:S(2)}, u32[]{:S(2)}) collective-permute-start(f32[4,2560]{1,0:T(4,128)S(1)} %slice.132), channel_id=1, source_target_pairs={{0,8},{4,12},{8,16},{12,20},{16,24},{20,28},{1,9},{5,13},{9,17},{1... | collective-permute-start | bytes 122888
  111.7 4.5 copy-start.1
  146.9 21.5 %copy-start.54 = (s32[8,1]{0,1:T(1,128)S(1)}, s32[8,1]{0,1:T(1,128)}, u32[]{:S(2)}) copy-start(s32[8,1]{0,1:T(1,128)} %get-tuple-element.46) | copy-start | bytes 100
  146.9 22.4 %copy-start.53 = (s32[8,1]{0,1:T(1,128)S(1)}, s32[8,1]{0,1:T(1,128)}, u32[]{:S(2)}) copy-start(s32[8,1]{0,1:T(1,128)} %get-tuple-element.45) | copy-start | bytes 100
  146.9 23.8 %copy-start.52 = (s32[8,1]{0,1:T(1,128)S(1)}, s32[8,1]{0,1:T(1,128)}, u32[]{:S(2)}) copy-start(s32[8,1]{0,1:T(1,128)} %get-tuple-element.44) | copy-start | bytes 100
  168.6 55.9 %copy-start.41 = (s32[8]{0:T(128)}, s32[8]{0:T(128)S(1)}, u32[]{:S(2)}) copy-start(s32[8]{0:T(128)S(1)} %add_bitcast_fusion.2) | copy-start | bytes 100
  171.7 5.5 copy-start.6
  171.7 5.5 copy-start.7
  177.2 3.2 copy-start.8
  177.2 4.4 copy-start.9
  181.6 3.2 copy-start.10
  181.6 4.4 copy-start.11
  186.0 3.5 copy-start.51
  199.4 16.9 %copy-start.13 = (bf16[1024,256]{1,0:T(8,128)(2,1)S(1)}, bf16[1024,256]{1,0:T(8,128)(2,1)}, u32[]{:S(2)}) copy-start(bf16[1024,256]{1,0:T(8,128)(2,1)} %param.33) | copy-start | bytes 1572868
  199.4 16.9 %copy-start.21 = (f32[1024]{0:T(1024)S(1)}, f32[1024]{0:T(1024)}, u32[]{:S(2)}) copy-start(f32[1024]{0:T(1024)} %param.32) | copy-start | bytes 12292
  199.4 17.6 %copy-start.50 = (u32[32]{0:T(128)S(1)}, u32[32]{0:T(128)}, u32[]{:S(2)}) copy-start(u32[32]{0:T(128)} %constant.111) | copy-start | bytes 388
  199.9 18.7 %copy-start.20 = (bf16[8,1024]{1,0:T(8,128)(2,1)S(1)}, bf16[8,1024]{1,0:T(8,128)(2,1)}, u32[]{:S(2)}) copy-start(bf16[8,1024]{1,0:T(8,128)(2,1)} %param.24) | copy-start | bytes 49156
  199.9 18.7 %copy-start.34 = (pred[8]{0:T(512)(128)(4,1)S(1)}, pred[8]{0:T(512)(128)(4,1)}, u32[]{:S(2)}) copy-start(pred[8]{0:T(512)(128)(4,1)} %copy-done.33) | copy-start | bytes 28
  199.9 18.7 %copy-start.40 = (s32[8]{0:T(128)S(1)}, s32[8]{0:T(128)}, u32[]{:S(2)}) copy-start(s32[8]{0:T(128)} %copy-done.39) | copy-start | bytes 100
  199.9 18.9 %copy-start.45 = (s32[8]{0:T(128)S(1)}, s32[8]{0:T(128)}, u32[]{:S(2)}) copy-start(s32[8]{0:T(128)} %get-tuple-element.49) | copy-start | bytes 100
  212.3 6.0 collective-permute-start.3
  214.3 4.0 collective-permute-start.2
  219.2 5.3 copy-start.32
  262.7 72.3 %copy-start.48 = (f32[8]{0:T(128)S(1)}, f32[8]{0:T(128)}, u32[]{:S(2)}) copy-start(f32[8]{0:T(128)} %get-tuple-element.88) | copy-start | bytes 100
  311.2 24.4 %collective-permute-start.4 = (f32[24,2560]{1,0:T(8,128)S(1)}, f32[24,2560]{1,0:T(8,128)}, u32[]{:S(2)}, u32[]{:S(2)}) collective-permute-start(f32[24,2560]{1,0:T(8,128)S(1)} %fusion.2), channel_id=1, source_target_pairs={{0,4},{4,8},{8,12},{12,16},{16,20},{20,24},{24,28},{1,5},{5,9},{9,... | collective-permute-start | bytes 737288
  317.4 18.1 %collective-permute-start.5 = (f32[4,2560]{1,0:T(4,128)S(1)}, f32[4,2560]{1,0:T(4,128)S(1)}, u32[]{:S(2)}, u32[]{:S(2)}) collective-permute-start(f32[4,2560]{1,0:T(4,128)S(1)} %slice.134), channel_id=1, source_target_pairs={{0,8},{4,12},{8,16},{12,20},{16,24},{20,28},{1,9},{5,13},{9,17},{1... | collective-permute-start | bytes 122888
  349.4 19.7 %copy-start.55 = (f32[8]{0:T(128)S(1)}, f32[8]{0:T(128)}, u32[]{:S(2)}) copy-start(f32[8]{0:T(128)} %add_rsqrt_fusion.7) | copy-start | bytes 100
  350.0 20.2 %copy-start.42 = (s32[8]{0:T(128)S(1)}, s32[8]{0:T(128)}, u32[]{:S(2)}) copy-start(s32[8]{0:T(128)} %copy-done.41) | copy-start | bytes 100
  350.0 20.4 %copy-start.44 = (s32[8]{0:T(128)S(1)}, s32[8]{0:T(128)}, u32[]{:S(2)}) copy-start(s32[8]{0:T(128)} %get-tuple-element.51) | copy-start | bytes 100
  363.5 6.4 collective-permute-start.7
  365.2 4.7 collective-permute-start.6
  370.7 5.4 copy-start.31
  370.7 5.3 copy-start.37
  415.3 72.3 %copy-start.49 = (f32[8]{0:T(128)S(1)}, f32[8]{0:T(128)}, u32[]{:S(2)}) copy-start(f32[8]{0:T(128)} %get-tuple-element.86) | copy-start | bytes 100
  463.7 24.4 %collective-permute-start.8 = (f32[24,2560]{1,0:T(8,128)S(1)}, f32[24,2560]{1,0:T(8,128)}, u32[]{:S(2)}, u32[]{:S(2)}) collective-permute-start(f32[24,2560]{1,0:T(8,128)S(1)} %fusion.4), channel_id=1, source_target_pairs={{0,4},{4,8},{8,12},{12,16},{16,20},{20,24},{24,28},{1,5},{5,9},{9,... | collective-permute-start | bytes 737288
  470.0 18.1 %collective-permute-start.9 = (f32[4,2560]{1,0:T(4,128)S(1)}, f32[4,2560]{1,0:T(4,128)S(1)}, u32[]{:S(2)}, u32[]{:S(2)}) collective-permute-start(f32[4,2560]{1,0:T(4,128)S(1)} %slice.136), channel_id=1, source_target_pairs={{0,8},{4,12},{8,16},{12,20},{16,24},{20,28},{1,9},{5,13},{9,17},{1... | collective-permute-start | bytes 122888
  501.9 17.8 %copy-start.56 = (f32[8]{0:T(128)S(1)}, f32[8]{0:T(128)}, u32[]{:S(2)}) copy-start(f32[8]{0:T(128)} %add_rsqrt_fusion.4) | copy-start | bytes 100
  502.5 18.6 %copy-start.38 = (s32[8]{0:T(128)S(1)}, s32[8]{0:T(128)}, u32[]{:S(2)}) copy-start(s32[8]{0:T(128)} %add_bitcast_fusion.1) | copy-start | bytes 100
  502.5 18.8 %copy-start.43 = (s32[8]{0:T(128)S(1)}, s32[8]{0:T(128)}, u32[]{:S(2)}) copy-start(s32[8]{0:T(128)} %get-tuple-element.48) | copy-start | bytes 100
  515.7 4.8 collective-permute-start.11
  517.8 3.1 collective-permute-start.10
  521.6 4.8 copy-start.29
  521.6 4.8 copy-start.35
  566.7 69.8 %copy-start.26 = (pred[20,256]{1,0:T(8,128)(4,1)S(1)}, pred[20,256]{1,0:T(8,128)(4,1)}, u32[]{:S(2)}) copy-start(pred[20,256]{1,0:T(8,128)(4,1)} %iota_compare_fusion) | copy-start | bytes 15364
  610.6 24.3 %collective-permute-start.12 = (f32[24,2560]{1,0:T(8,128)S(1)}, f32[24,2560]{1,0:T(8,128)}, u32[]{:S(2)}, u32[]{:S(2)}) collective-permute-start(f32[24,2560]{1,0:T(8,128)S(1)} %fusion.6), channel_id=1, source_target_pairs={{0,4},{4,8},{8,12},{12,16},{16,20},{20,24},{24,28},{1,5},{5,9},{9,... | collective-permute-start | bytes 737288
  616.9 18.0 %collective-permute-start.13 = (f32[4,2560]{1,0:T(4,128)S(1)}, f32[4,2560]{1,0:T(4,128)S(1)}, u32[]{:S(2)}, u32[]{:S(2)}) collective-permute-start(f32[4,2560]{1,0:T(4,128)S(1)} %slice.138), channel_id=1, source_target_pairs={{0,8},{4,12},{8,16},{12,20},{16,24},{20,28},{1,9},{5,13},{9,17},{1... | collective-permute-start | bytes 122888
  641.9 17.7 %copy-start.23 = (f32[8,1,256]{2,0,1:T(8,128)S(1)}, f32[8,1,256]{2,0,1:T(8,128)}, u32[]{:S(2)}) copy-start(f32[8,1,256]{2,0,1:T(8,128)} %convolution_bitcast_fusion.3) | copy-start | bytes 24580
  641.9 17.7 %copy-start.24 = (f32[8,1,256]{2,0,1:T(8,128)S(1)}, f32[8,1,256]{2,0,1:T(8,128)}, u32[]{:S(2)}) copy-start(f32[8,1,256]{2,0,1:T(8,128)} %convolution_bitcast_fusion.2) | copy-start | bytes 24580
  641.9 17.7 %copy-start.25 = (f32[8,1,256]{2,0,1:T(8,128)S(1)}, f32[8,1,256]{2,0,1:T(8,128)}, u32[]{:S(2)}) copy-start(f32[8,1,256]{2,0,1:T(8,128)} %convolution_bitcast_fusion.1) | copy-start | bytes 24580
  642.0 19.1 %copy-start.30 = (pred[8]{0:T(512)(128)(4,1)S(1)}, pred[8]{0:T(512)(128)(4,1)}, u32[]{:S(2)}) copy-start(pred[8]{0:T(512)(128)(4,1)} %get-tuple-element.40) | copy-start | bytes 28
  642.0 19.1 %copy-start.36 = (s32[8]{0:T(128)S(1)}, s32[8]{0:T(128)}, u32[]{:S(2)}) copy-start(s32[8]{0:T(128)} %add_bitcast_fusion) | copy-start | bytes 100
  655.7 4.6 collective-permute-start.15
  657.7 3.1 collective-permute-start.14
  (9 other events, 15.7 us)
where the time goes:
time: 667 us; the launch traced here: 662 us
  blocking collectives  427 us (64%)
  local copies, waits for them, and re-layouts  77.4 us (12%)
  matrix products  71 us (11%)
  starting transfers between devices  54.8 us (8%)
  other arithmetic  28.1 us (4%)
    unnamed x8, blocking collectives  224 us
    all_gather x4, blocking collectives, on_device(): all_slots = lax.all_gather(slot_h, ('rows', 'tp'), axis=0, tiled=True)  142 us
    psum x4, blocking collectives, on_device(): sq_total = lax.psum(jnp.sum(upper * upper, axis=1), 'rows')  60.3 us
    unnamed x16, starting transfers between devices  54.8 us
    unnamed x151, local copies, waits for them, and re-layouts  30.2 us
    dot_general x4, matrix products, on_device(): state = x_val + jnp.dot(inner, w_out, preferred_element_type=jnp.float32)  20.3 us
    dot_general x4, matrix products, on_device(): jnp.dot(normed, w_qkv, preferred_element_type=jnp.float32)  18.9 us
    gather x4, local copies, waits for them, and re-layouts, on_device(): jnp.take(value_cache, row_index, axis=0)  18.3 us
  transfers between devices with their start and end apart: 16, of which 2 were waited for; matrix products, arithmetic and copies ran while one was open for 10% of the time, Pallas kernels for 0%

commit v1 on v0

v1 whole, which is shorter than its diff:
```python
import functools

import jax
import jax.numpy as jnp
import numpy as np
from jax import lax
from jax.experimental import pallas as pl
from jax.experimental.pallas import tpu as pltpu
from jax.sharding import PartitionSpec as P

HD = 128
CAP = 5
R_DEV = 8
EPS = 1e-05
MESH = pl.DeviceIdType.MESH
F32 = jnp.float32
BF16 = jnp.bfloat16


def rms_scale(values, gain):
    mean_sq = jnp.mean(values * values, axis=-1, keepdims=True)
    return values * lax.rsqrt(mean_sq + EPS) * gain


def slot_picker(finished):
    ranked = jnp.cumsum(finished, axis=-1) - 1
    slot_ids = jnp.arange(CAP, dtype=jnp.int32)
    chosen = (finished[..., None, :] == 1) & (ranked[..., None, :] == slot_ids[:, None])
    return chosen.astype(jnp.int32)


def unpack_matrix():
    m = np.zeros((384, 256), np.float32)
    for d in range(16):
        for k in range(4):
            for c in range(4):
                m[k * 64 + d * 4 + c, d * 16 + 4 * k + c] = 1
        for k in range(8):
            m[256 + k * 16 + d, d * 16 + k] = 1
    return m


def dot(a, b):
    return jnp.dot(a, b, preferred_element_type=F32)


def kernel(
    n_rows, n_tp, n_steps,
    idx_ref, len_ref, hidden_ref, context_ref, oh_ref, pick_ref, pickt_ref, unpack_ref,
    gl_ref, og_ref, gg_ref,
    embed_hbm, w_in_hbm, w_out_hbm, w_vocab_hbm, w_up_hbm, w_q_hbm, w_k_hbm, w_v_hbm,
    kc_hbm, vc_hbm, w_mix_hbm,
    logits_ref, ctx_out_ref,
    embed, w_in, w_out, w_vocab, w_up, w_q, w_k, w_v, kc, vc, w_mix,
    emb_s, state_s, ctx_s, packm, packt, ag_send, ag_recv, h_s,
    qs_main, tail_f, qs_tail, qr_main, qr_tail, ss_send, ss_recv,
    qf, tsum, scores, selfs, probs, owns, of, mix_s, tp_recv,
    load_sem, ag_ssem, ag_rsem, q_ssem, q_rsem, tp_ssem, tp_rsem,
):
    r = lax.axis_index("rows")
    t = lax.axis_index("tp")
    n_dev = n_rows * n_tp
    me = r * n_tp + t
    dl = hidden_ref.shape[1]
    q_cols, kv_cols = w_q.shape[1], w_k.shape[1]
    cols = q_cols + 2 * kv_cols
    kv_local = kv_cols // HD
    n_heads = q_cols // HD
    group = n_heads // kv_local
    n_main, n_tail = 4 * n_dev, n_dev
    g_main, g_tail = 4 * n_tp, n_tp
    chunks = 16 // n_tp
    cw = cols // chunks
    hs = -(-(CAP * n_tp) // 8) * 8
    vocab = w_vocab.shape[1]
    dg = n_rows * w_up.shape[1]
    scale = 1.0 / np.float32(np.sqrt(np.float32(HD)))

    loads = [
        pltpu.make_async_copy(a, b, load_sem.at[i])
        for i, (a, b) in enumerate(
            [
                (embed_hbm, embed), (w_in_hbm, w_in), (w_out_hbm, w_out),
                (w_vocab_hbm, w_vocab), (w_up_hbm, w_up), (w_q_hbm, w_q),
                (w_k_hbm, w_k), (w_v_hbm, w_v), (kc_hbm, kc), (vc_hbm, vc),
                (w_mix_hbm, w_mix),
            ]
        )
    ]
    for c in loads:
        c.start()

    barrier = pltpu.get_barrier_semaphore()

    def greet(i, carry):
        to = lax.rem(me + i, n_dev)
        pl.semaphore_signal(
            barrier, inc=1, device_id=(to // n_tp, lax.rem(to, n_tp)), device_id_type=MESH
        )
        return carry

    lax.fori_loop(1, n_dev, greet, 0)

    state_s[...] = hidden_ref[...].astype(F32)
    ctx_s[...] = context_ref[...].astype(F32)
    ss_send[...] = jnp.zeros_like(ss_send)
    of[...] = jnp.zeros_like(of)
    packt[...] = jnp.zeros_like(packt)
    loads[0].wait()
    emb_s[...] = dot(oh_ref[...], embed[...])
    pl.semaphore_wait(barrier, n_dev - 1)

    def ag_copy(s, to, src):
        return pltpu.make_async_remote_copy(
            src_ref=ag_send,
            dst_ref=ag_recv.at[s, pl.ds(pl.multiple_of(src * 16, 16), 16)],
            send_sem=ag_ssem.at[to],
            recv_sem=ag_rsem.at[s, src],
            device_id=(to // n_tp, lax.rem(to, n_tp)),
            device_id_type=MESH,
        )

    def q_copies(s, to, src):
        return [
            pltpu.make_async_remote_copy(
                src_ref=a.at[pl.ds(pl.multiple_of(to * rows, rows), rows)],
                dst_ref=b.at[s, pl.ds(pl.multiple_of(src * rows, rows), rows)],
                send_sem=q_ssem.at[i, to],
                recv_sem=q_rsem.at[s, i, src],
                device_id=(to, t),
                device_id_type=MESH,
            )
            for i, (a, b, rows) in enumerate(
                [(qs_main, qr_main, g_main), (qs_tail, qr_tail, 16), (ss_send, ss_recv, hs)]
            )
        ]

    def tp_copy(s, to, src):
        return pltpu.make_async_remote_copy(
            src_ref=mix_s.at[pl.ds(pl.multiple_of(to * 8, 8), 8)],
            dst_ref=tp_recv.at[s, pl.ds(pl.multiple_of(src * 8, 8), 8)],
            send_sem=tp_ssem.at[to],
            recv_sem=tp_rsem.at[s, src],
            device_id=(r, to),
            device_id_type=MESH,
        )

    def step(s, carry):
        s8 = pl.multiple_of(s * 8, 8)
        x = state_s[...] + emb_s[pl.ds(s8, 8), :] + ctx_s[...]
        a = rms_scale(x, gl_ref[...]).astype(BF16)

        @pl.when(s == 0)
        def _():
            loads[1].wait()
            loads[2].wait()

        f = dot(a, w_in[...])
        f = (f / (1.0 + jnp.exp(-f))).astype(BF16)
        state = x + dot(f, w_out[...])
        state_s[...] = state
        slots = dot(pick_ref[s].astype(BF16), state.astype(BF16))
        for k in range(4):
            w = dl // 4
            packm[4 * k : 4 * k + 4, :] = slots[0:4, w * k : w * k + w]
        for k in range(8):
            w = dl // 8
            packt[k : k + 1, :] = slots[4:5, w * k : w * k + w]
        packed = jnp.concatenate([packm[...], packt[...]], axis=1).astype(BF16)
        ag_send[...] = packed

        def send(i, c):
            ag_copy(s, lax.rem(me + i, n_dev), me).start()
            return c

        lax.fori_loop(1, n_dev, send, 0)
        ag_recv[s, pl.ds(pl.multiple_of(me * 16, 16), 16), :] = packed

        @pl.when(s == 0)
        def _():
            loads[3].wait()
            loads[4].wait()

        final = rms_scale(state, og_ref[...]).astype(BF16)
        logits_ref[:, pl.ds(pl.multiple_of(s * vocab, vocab), vocab)] = dot(final, w_vocab[...])

        def recv(i, c):
            src = lax.rem(me + n_dev - i, n_dev)
            ag_copy(s, me, src).wait_recv()
            return c

        lax.fori_loop(1, n_dev, recv, 0)

        for g in range(n_dev // 16):
            got = ag_recv[s, g * 256 : g * 256 + 256, :]
            m = dot(unpack_ref[0:256, :], got[:, 0:256]).astype(BF16)
            tl = dot(unpack_ref[256:384, :], got[:, 256:384]).astype(BF16)
            for k in range(4):
                h_s[g * 64 : g * 64 + 64, 256 * k : 256 * k + 256] = m[k * 64 : k * 64 + 64]
            for k in range(8):
                h_s[n_main + g * 16 : n_main + g * 16 + 16, 128 * k : 128 * k + 128] = tl[
                    k * 16 : k * 16 + 16
                ]
        up = dot(h_s[...], w_up[...])
        ss = jnp.broadcast_to(jnp.sum(up * up, axis=1, keepdims=True), (up.shape[0], 128))
        for g in range(n_rows):
            ss_send[g * hs : g * hs + g_main, :] = ss[g * g_main : (g + 1) * g_main]
            ss_send[g * hs + g_main : g * hs + g_main + g_tail, :] = ss[
                n_main + g * g_tail : n_main + (g + 1) * g_tail
            ]
        normed = (up * gg_ref[...].astype(F32)).astype(BF16)

        @pl.when(s == 0)
        def _():
            loads[5].wait()
            loads[6].wait()
            loads[7].wait()

        q = dot(normed, w_q[...])
        kv = jnp.concatenate([dot(normed, w_k[...]), dot(normed, w_v[...])], axis=1)
        qs_main[:, 0:q_cols] = q[0:n_main].astype(BF16)
        qs_main[:, q_cols:cols] = kv[0:n_main].astype(BF16)
        tail = jnp.concatenate([q[n_main:], kv[n_main:]], axis=1)
        for g in range(n_rows):
            for k in range(chunks):
                at = g * 16 + k * n_tp
                tail_f[at : at + n_tp, :] = tail[g * n_tp : (g + 1) * n_tp, cw * k : cw * k + cw]
        qs_tail[...] = tail_f[...].astype(BF16)

        def qsend(i, c):
            for copy in q_copies(s, lax.rem(r + i, n_rows), r):
                copy.start()
            return c

        lax.fori_loop(1, n_rows, qsend, 0)
        for a_ref, b_ref, rows in (
            (qs_main, qr_main, g_main), (qs_tail, qr_tail, 16), (ss_send, ss_recv, hs)
        ):
            at = pl.ds(pl.multiple_of(r * rows, rows), rows)
            b_ref[s, at, :] = a_ref[at, :]

        def qrecv(i, c):
            for copy in q_copies(s, r, lax.rem(r + n_rows - i, n_rows)):
                copy.wait_recv()
            return c

        lax.fori_loop(1, n_rows, qrecv, 0)

        inv = ss_recv[s, 0:hs, :]
        tsum_v = qr_tail[s, 0:16, :].astype(F32)
        for g in range(1, n_rows):
            inv = inv + ss_recv[s, g * hs : (g + 1) * hs, :]
            tsum_v = tsum_v + qr_tail[s, g * 16 : (g + 1) * 16, :].astype(F32)
        inv = lax.rsqrt(inv * (1.0 / dg) + EPS)
        tsum[...] = tsum_v
        for h in range(cols // HD):
            at = slice(h * HD, (h + 1) * HD)
            v = qr_main[s, 0:g_main, at].astype(F32)
            for g in range(1, n_rows):
                v = v + qr_main[s, g * g_main : (g + 1) * g_main, at].astype(F32)
            qf[h * hs : h * hs + g_main, :] = (v * inv[0:g_main]).astype(BF16).astype(F32)
            k, off = (h * HD) // cw, (h * HD) % cw
            tv = tsum[k * n_tp : (k + 1) * n_tp, off : off + HD]
            qf[h * hs + g_main : h * hs + g_main + g_tail, :] = (
                (tv * inv[g_main : g_main + g_tail]).astype(BF16).astype(F32)
            )

        @pl.when(s == 0)
        def _():
            loads[8].wait()
            loads[9].wait()
            loads[10].wait()

        positions = lax.broadcasted_iota(jnp.int32, (group, kc.shape[1]), 1)
        n_slots = n_tp * CAP
        pairs = []
        for tt in range(n_tp):
            for c in range(CAP):
                j = tt * 4 + c if c < 4 else g_main + tt
                for v in range(kv_local):
                    pairs.append((tt, c, j, v))
        for p, (tt, c, j, v) in enumerate(pairs):
            row = idx_ref[s * n_slots + tt * CAP + c]
            length = len_ref[s * n_slots + tt * CAP + c]
            q8 = qf[pl.ds(v * group * hs + j, group, stride=hs), :]
            nk = qf[pl.ds((n_heads + v) * hs + j, 1), :]
            keys = kc[row, :, v * HD : (v + 1) * HD]
            sc = lax.dot_general(
                q8.astype(BF16), keys, (((1,), (1,)), ((), ())), preferred_element_type=F32
            )
            scores[p * group : (p + 1) * group, :] = jnp.where(
                positions < length, sc * scale, -jnp.inf
            )
            selfs[p * group : (p + 1) * group, :] = jnp.broadcast_to(
                jnp.sum(q8 * nk, axis=1, keepdims=True) * scale, (group, 128)
            )
        sc = scores[...]
        own = selfs[:, 0:1]
        top = jnp.maximum(jnp.max(sc, axis=1, keepdims=True), own)
        w = jnp.exp(sc - top)
        wo = jnp.exp(own - top)
        inv_total = 1.0 / (jnp.sum(w, axis=1, keepdims=True) + wo)
        probs[...] = (w * inv_total).astype(BF16).astype(F32)
        owns[...] = jnp.broadcast_to((wo * inv_total).astype(BF16).astype(F32), owns.shape)
        os = n_tp * 8
        for p, (tt, c, j, v) in enumerate(pairs):
            row = idx_ref[s * n_slots + tt * CAP + c]
            nv = qf[pl.ds((n_heads + kv_local + v) * hs + j, 1), :]
            values = vc[row, :, v * HD : (v + 1) * HD]
            pr = probs[p * group : (p + 1) * group, :].astype(BF16)
            o = dot(pr, values) + owns[p * group : (p + 1) * group, :] * nv
            of[pl.ds(v * group * os + tt * 8 + c, group, stride=os), :] = o

        att = jnp.concatenate(
            [of[h * os : (h + 1) * os, :].astype(BF16) for h in range(n_heads)], axis=1
        )
        mix_s[...] = dot(att, w_mix[...])

        def tsend(i, c):
            tp_copy(s, lax.rem(t + i, n_tp), t).start()
            return c

        lax.fori_loop(1, n_tp, tsend, 0)
        at = pl.ds(pl.multiple_of(t * 8, 8), 8)
        tp_recv[s, at, :] = mix_s[at, :]

        def trecv(i, c):
            tp_copy(s, t, lax.rem(t + n_tp - i, n_tp)).wait_recv()
            return c

        lax.fori_loop(1, n_tp, trecv, 0)
        patch = tp_recv[s, 0:8, :]
        for g in range(1, n_tp):
            patch = patch + tp_recv[s, g * 8 : (g + 1) * 8, :]
        back = pickt_ref[s]
        delivered = dot(back.astype(BF16), patch.astype(BF16))
        done = jnp.sum(back, axis=1, keepdims=True) > 0.0
        ctx_s[...] = jnp.where(done, delivered, ctx_s[...])

        def drain_ag(i, c):
            ag_copy(s, lax.rem(me + i, n_dev), me).wait_send()
            return c

        def drain_q(i, c):
            for copy in q_copies(s, lax.rem(r + i, n_rows), r):
                copy.wait_send()
            return c

        def drain_tp(i, c):
            tp_copy(s, lax.rem(t + i, n_tp), t).wait_send()
            return c

        lax.fori_loop(1, n_dev, drain_ag, 0)
        lax.fori_loop(1, n_rows, drain_q, 0)
        lax.fori_loop(1, n_tp, drain_tp, 0)
        return carry

    lax.fori_loop(0, n_steps, step, 0)
    ctx_out_ref[...] = ctx_s[...].astype(BF16)


def on_device(
    hidden, context, byte_input_codes, finish, cache_len, embed, gain_local, w_in, w_out,
    output_norm_gain, w_vocab, w_up, gain_global, w_query, w_key, w_value, key_cache,
    value_cache, w_mix,
):
    n_rows, n_tp = lax.axis_size("rows"), lax.axis_size("tp")
    t = lax.axis_index("tp")
    rows, dl = hidden.shape
    n_steps = byte_input_codes.shape[1]
    vocab = embed.shape[0]
    n_dev = n_rows * n_tp
    slots = n_tp * CAP
    q_cols, kv_cols = w_query.shape[1], w_key.shape[1]
    cols = q_cols + 2 * kv_cols
    hs = -(-slots // 8) * 8
    cache = key_cache.shape[1]
    n_heads = q_cols // HD
    att_rows = slots * n_heads
    cw = cols * n_tp // 16

    oh = (
        byte_input_codes.T.reshape(n_steps * rows, 1) == jnp.arange(vocab, dtype=jnp.int32)[None, :]
    ).astype(BF16)
    picker = slot_picker(finish.T.reshape(n_steps, n_tp, rows))
    local = jnp.sum(picker * jnp.arange(rows, dtype=jnp.int32), axis=-1)
    row_index = (local + jnp.arange(n_tp, dtype=jnp.int32)[:, None] * rows).reshape(-1)
    lengths = jnp.take(cache_len, row_index, axis=0)
    mine = lax.dynamic_index_in_dim(picker, t, 1, keepdims=False).astype(F32)
    pick = jnp.pad(mine, ((0, 0), (0, 8 - CAP), (0, 0)))
    pickt = pick.transpose(0, 2, 1)

    vm = pl.BlockSpec(memory_space=pltpu.VMEM)
    sm = pl.BlockSpec(memory_space=pltpu.SMEM)
    anys = pl.BlockSpec(memory_space=pl.ANY)
    weights = (
        embed, w_in, w_out, w_vocab, w_up, w_query, w_key, w_value, key_cache, value_cache, w_mix
    )
    dma = pltpu.SemaphoreType.DMA
    logits, ctx = pl.pallas_call(
        functools.partial(kernel, n_rows, n_tp, n_steps),
        out_shape=(
            jax.ShapeDtypeStruct((rows, n_steps * vocab), F32),
            jax.ShapeDtypeStruct((rows, dl), BF16),
        ),
        in_specs=[sm, sm] + [vm] * 9 + [anys] * len(weights),
        out_specs=(vm, vm),
        scratch_shapes=[pltpu.VMEM(w.shape, w.dtype) for w in weights]
        + [
            pltpu.VMEM((n_steps * rows, dl), F32),
            pltpu.VMEM((rows, dl), F32),
            pltpu.VMEM((rows, dl), F32),
            pltpu.VMEM((16, dl // 4), F32),
            pltpu.VMEM((16, dl // 8), F32),
            pltpu.VMEM((16, 3 * dl // 8), BF16),
            pltpu.VMEM((n_steps, n_dev * 16, 3 * dl // 8), BF16),
            pltpu.VMEM((5 * n_dev, dl), BF16),
            pltpu.VMEM((4 * n_dev, cols), BF16),
            pltpu.VMEM((16 * n_rows, cw), F32),
            pltpu.VMEM((16 * n_rows, cw), BF16),
            pltpu.VMEM((n_steps, 4 * n_dev, cols), BF16),
            pltpu.VMEM((n_steps, 16 * n_rows, cw), BF16),
            pltpu.VMEM((n_rows * hs, 128), F32),
            pltpu.VMEM((n_steps, n_rows * hs, 128), F32),
            pltpu.VMEM((cols // HD * hs, HD), F32),
            pltpu.VMEM((16, cw), F32),
            pltpu.VMEM((att_rows, cache), F32),
            pltpu.VMEM((att_rows, 128), F32),
            pltpu.VMEM((att_rows, cache), F32),
            pltpu.VMEM((att_rows, 128), F32),
            pltpu.VMEM((n_heads * n_tp * 8, HD), F32),
            pltpu.VMEM((n_tp * 8, dl), F32),
            pltpu.VMEM((n_steps, n_tp * 8, dl), F32),
            dma((len(weights),)),
            dma((n_dev,)),
            dma((n_steps, n_dev)),
            dma((3, n_rows)),
            dma((n_steps, 3, n_rows)),
            dma((n_tp,)),
            dma((n_steps, n_tp)),
        ],
        compiler_params=pltpu.CompilerParams(
            collective_id=0, has_side_effects=True, vmem_limit_bytes=56 * 1024 * 1024
        ),
    )(
        row_index, lengths, hidden, context, oh, pick, pickt,
        jnp.asarray(unpack_matrix(), BF16),
        gain_local.reshape(1, -1), output_norm_gain.reshape(1, -1), gain_global.reshape(1, -1),
        *weights,
    )
    return logits.reshape(rows, n_steps, vocab), ctx


def solution(mesh):
    in_specs = (
        P(("rows", "tp"), None),
        P(("rows", "tp"), None),
        P(("rows", "tp"), None),
        P("rows", None),
        P("rows"),
        P(),
        P(),
        P(),
        P(),
        P(),
        P(),
        P(None, "rows"),
        P("rows"),
        P("rows", "tp"),
        P("rows", "tp"),
        P("rows", "tp"),
        P("rows", None, "tp"),
        P("rows", None, "tp"),
        P("tp", None),
    )
    out_specs = (P(("rows", "tp"), None, None), P(("rows", "tp"), None))
    return jax.shard_map(
        on_device, mesh=mesh, in_specs=in_specs, out_specs=out_specs, check_vma=False
    )
```

time: 667 us -> 180 us (0.27)
  blocking collectives: 427 us -> 0 us
  Pallas kernels: 0 us -> 169 us
  matrix products: 71 us -> 0 us
  local copies, waits for them, and re-layouts: 77.4 us -> 8.28 us
  starting transfers between devices: 54.8 us -> 0 us
  other arithmetic: 28.1 us -> 2.24 us
    unnamed x8 -> x0, blocking collectives: 224 us -> none
    pallas_call x0 -> x1, Pallas kernels: none -> 169 us  [on_device(): pl.pallas_call(functools.partial(kernel, n_rows, n_tp, n_steps), out_shap...]
    all_gather x4 -> x0, blocking collectives: 142 us -> none  [on_device(): all_slots = lax.all_gather(slot_h, ('rows', 'tp'), axis=0, tiled=True)]
    dot_general x44 -> x0, matrix products: 71 us -> none  [the longest x4 20.3 us: on_device(): state = x_val + jnp.dot(inner, w_out, preferred_element_type=jnp.float32)]
    psum x4 -> x0, blocking collectives: 60.3 us -> none  [on_device(): sq_total = lax.psum(jnp.sum(upper * upper, axis=1), 'rows')]
    unnamed x16 -> x0, starting transfers between devices: 54.8 us -> none
    gather x8 -> x0, local copies, waits for them, and re-layouts: 36.5 us -> none  [the longest x4 18.3 us: on_device(): jnp.take(value_cache, row_index, axis=0)]
    unnamed x151 -> x7, local copies, waits for them, and re-layouts: 30.2 us -> 2.82 us
  transfers between devices with their start and end apart: 16 -> 0, of which waited for: 2 -> 0; matrix products, arithmetic and copies ran while one was open for 10% -> 0% of each run, Pallas kernels for 0% -> 0%
where the time goes in v1:
time: 180 us
  Pallas kernels  169 us (94%)
  local copies, waits for them, and re-layouts  8.28 us (5%)
  other arithmetic  2.24 us (1%)
    pallas_call x1, Pallas kernels, on_device(): pl.pallas_call(functools.partial(kernel, n_rows, n_tp, n_steps), out_shap...  169 us

profile of v1, /device:TPU:11, one launch (start us, length us, event | category | flops | bytes accessed | tf_op | source)
XLA Modules:
  0.0 180.0 jit_solution(11670497268750913286)
XLA Ops:
  0.6 0.0 copy-start
  0.6 0.8 eq.44
  1.4 1.3 reshape.82.gg_ref
  2.7 0.8 broadcast_in_dim_reshape.3
  3.5 0.7 reduce_window_sum.11
  4.2 0.1 select_reduce_fusion
  4.3 0.1 broadcast_add_fusion
  4.4 0.1 add.58.idx_ref
  4.5 0.0 copy-start.1
  4.5 0.1 add.61
  4.6 0.0 copy-done
  4.7 1.2 gather_fusion
  5.9 0.5 and_select_fusion.len_ref
  6.4 0.1 fusion
  6.5 0.7 fusion.1.oh_ref
  7.2 0.6 pad_bitcast_fusion.pickt_ref
  7.8 0.1 copy.36
  7.9 0.6 pad.4.clone.pick_ref
  8.5 0.0 copy-done.1
  8.5 168.8 %shard_map.203 = (f32[8,1024]{1,0:T(8,128)}, bf16[8,1024]{1,0:T(8,128)(2,1)}) custom-call(s32[80]{0:T(128)} %copy-done.1, s32[80]{0:T(128)} %and_select_fusion.len_ref, bf16[8,1024]{1,0:T(8,128)(2,1)} %hidden_ref.1, bf16[8,1024]{1,0:T(8,128)(2,1)} %context_ref.1, bf16[32,256]{1,0:T(8,128)(2,1)} %fusion.1.oh_ref, f32[4,8,8]{2,1,0:T(8,128)} %pad.4.clone.pick_ref, ...), custom_call_target="tpu_custom_call" | custom-call | tf_op jit(solution)/shard_map/pallas_call | solution.py:400
  177.3 1.4 copy.35
  178.7 1.3 copy.38
  (9 shorter events, 0.1 us)
Async XLA Ops:
  0.6 4.0 %copy-start = (s32[32]{0:T(128)S(1)}, s32[32]{0:T(128)}, u32[]{:S(2)}) copy-start(s32[32]{0:T(128)} %param.24) | copy-start | bytes 388
  4.5 4.0 %copy-start.1 = (s32[80]{0:T(128)}, s32[80]{0:T(128)S(1)}, u32[]{:S(2)}) copy-start(s32[80]{0:T(128)S(1)} %add.58.idx_ref) | copy-start | bytes 964

commit v2 on v1

--- a/solution.py
+++ b/solution.py
@@ -53,9 +53,10 @@
     logits_ref, ctx_out_ref,
     embed, w_in, w_out, w_vocab, w_up, w_q, w_k, w_v, kc, vc, w_mix,
     emb_s, state_s, ctx_s, packm, packt, ag_send, ag_recv, h_s,
-    qs_main, tail_f, qs_tail, qr_main, qr_tail, ss_send, ss_recv,
+    qs_main, tail_f, qs_tail, xr_main, xr_tail, ys_main, ys_tail, qr_main, qr_tail, ss_send, ss_recv,
     qf, tsum, scores, selfs, probs, owns, of, mix_s, tp_recv,
-    load_sem, ag_ssem, ag_rsem, q_ssem, q_rsem, tp_ssem, tp_rsem,
+    load_sem, ag_ssem, fw_ssem, ag_rsem, x_ssem, x_rsem, z_ssem, z_rsem, n_ssem, n_rsem,
+    tp_ssem, tp_rsem,
 ):
     r = lax.axis_index("rows")
     t = lax.axis_index("tp")
@@ -72,6 +73,9 @@
     chunks = 16 // n_tp
     cw = cols // chunks
     hs = -(-(CAP * n_tp) // 8) * 8
+    outer = min(4, n_rows)
+    inner = n_rows // outer
+    hi, lo = r // inner, lax.rem(r, inner)
     vocab = w_vocab.shape[1]
     dg = n_rows * w_up.shape[1]
     scale = 1.0 / np.float32(np.sqrt(np.float32(HD)))
@@ -110,30 +114,77 @@
     emb_s[...] = dot(oh_ref[...], embed[...])
     pl.semaphore_wait(barrier, n_dev - 1)
 
-    def ag_copy(s, to, src):
+    def ag_rows(s, to, src):
+        slot = src * n_tp + t
         return pltpu.make_async_remote_copy(
             src_ref=ag_send,
-            dst_ref=ag_recv.at[s, pl.ds(pl.multiple_of(src * 16, 16), 16)],
+            dst_ref=ag_recv.at[s, pl.ds(pl.multiple_of(slot * 16, 16), 16)],
             send_sem=ag_ssem.at[to],
-            recv_sem=ag_rsem.at[s, src],
-            device_id=(to // n_tp, lax.rem(to, n_tp)),
-            device_id_type=MESH,
-        )
-
-    def q_copies(s, to, src):
-        return [
-            pltpu.make_async_remote_copy(
-                src_ref=a.at[pl.ds(pl.multiple_of(to * rows, rows), rows)],
-                dst_ref=b.at[s, pl.ds(pl.multiple_of(src * rows, rows), rows)],
-                send_sem=q_ssem.at[i, to],
-                recv_sem=q_rsem.at[s, i, src],
-                device_id=(to, t),
-                device_id_type=MESH,
-            )
-            for i, (a, b, rows) in enumerate(
-                [(qs_main, qr_main, g_main), (qs_tail, qr_tail, 16), (ss_send, ss_recv, hs)]
-            )
-        ]
+            recv_sem=ag_rsem.at[s, slot],
+            device_id=(to, t),
+            device_id_type=MESH,
+        )
+
+    def ag_own(s, to, src):
+        slot = r * n_tp + src
+        return pltpu.make_async_remote_copy(
+            src_ref=ag_send,
+            dst_ref=ag_recv.at[s, pl.ds(pl.multiple_of(slot * 16, 16), 16)],
+            send_sem=fw_ssem.at[r, to],
+            recv_sem=ag_rsem.at[s, slot],
+            device_id=(r, to),
+            device_id_type=MESH,
+        )
+
+    def ag_forward(s, row, to, src):
+        slot = row * n_tp + src
+        at = pl.ds(pl.multiple_of(slot * 16, 16), 16)
+        return pltpu.make_async_remote_copy(
+            src_ref=ag_recv.at[s, at],
+            dst_ref=ag_recv.at[s, at],
+            send_sem=fw_ssem.at[row, to],
+            recv_sem=ag_rsem.at[s, slot],
+            device_id=(r, to),
+            device_id_type=MESH,
+        )
+
+    def x_copy(s, p, to, src):
+        if p < chunks:
+            a, b, rows = qs_main.at[p], xr_main.at[s, p], outer * g_main
+        else:
+            a, b, rows = qs_tail, xr_tail.at[s], outer * 16
+        return pltpu.make_async_remote_copy(
+            src_ref=a.at[pl.ds(pl.multiple_of(to * rows, 16), rows)],
+            dst_ref=b.at[src],
+            send_sem=x_ssem.at[p, to],
+            recv_sem=x_rsem.at[s, p, src],
+            device_id=(hi * inner + to, t),
+            device_id_type=MESH,
+        )
+
+    def z_copy(s, p, to, src):
+        if p < chunks:
+            a, b, rows = ys_main.at[p], qr_main.at[s, p], g_main
+        else:
+            a, b, rows = ys_tail, qr_tail.at[s], 16
+        return pltpu.make_async_remote_copy(
+            src_ref=a.at[pl.ds(pl.multiple_of(to * rows, 16), rows)],
+            dst_ref=b.at[src],
+            send_sem=z_ssem.at[p, to],
+            recv_sem=z_rsem.at[s, p, src],
+            device_id=(to * inner + lo, t),
+            device_id_type=MESH,
+        )
+
+    def n_copy(s, to, src):
+        return pltpu.make_async_remote_copy(
+            src_ref=ss_send.at[pl.ds(pl.multiple_of(to * hs, 8), hs)],
+            dst_ref=ss_recv.at[s, pl.ds(pl.multiple_of(src * hs, 8), hs)],
+            send_sem=n_ssem.at[to],
+            recv_sem=n_rsem.at[s, src],
+            device_id=(to, t),
+            device_id_type=MESH,
+        )
 
     def tp_copy(s, to, src):
         return pltpu.make_async_remote_copy(
@@ -170,11 +221,25 @@
         ag_send[...] = packed
 
         def send(i, c):
-            ag_copy(s, lax.rem(me + i, n_dev), me).start()
-            return c
-
-        lax.fori_loop(1, n_dev, send, 0)
+            ag_rows(s, lax.rem(r + i, n_rows), r).start()
+            return c
+
+        def send_own(i, c):
+            ag_own(s, lax.rem(t + i, n_tp), t).start()
+            return c
+
+        lax.fori_loop(1, n_rows, send, 0)
+        lax.fori_loop(1, n_tp, send_own, 0)
         ag_recv[s, pl.ds(pl.multiple_of(me * 16, 16), 16), :] = packed
+
+        def forward(i, c):
+            row = lax.rem(r + n_rows - i, n_rows)
+            ag_rows(s, r, row).wait_recv()
+            for k in range(1, n_tp):
+                ag_forward(s, row, lax.rem(t + k, n_tp), t).start()
+            return c
+
+        lax.fori_loop(1, n_rows, forward, 0)
 
         @pl.when(s == 0)
         def _():
@@ -185,11 +250,15 @@
         logits_ref[:, pl.ds(pl.multiple_of(s * vocab, vocab), vocab)] = dot(final, w_vocab[...])
 
         def recv(i, c):
-            src = lax.rem(me + n_dev - i, n_dev)
-            ag_copy(s, me, src).wait_recv()
-            return c
-
-        lax.fori_loop(1, n_dev, recv, 0)
+            src = lax.rem(t + n_tp - i, n_tp)
+
+            def recv_row(row, c):
+                ag_forward(s, row, t, src).wait_recv()
+                return c
+
+            return lax.fori_loop(0, n_rows, recv_row, c)
+
+        lax.fori_loop(1, n_tp, recv, 0)
 
         for g in range(n_dev // 16):
             got = ag_recv[s, g * 256 : g * 256 + 256, :]
@@ -216,50 +285,76 @@
             loads[6].wait()
             loads[7].wait()
 
-        q = dot(normed, w_q[...])
-        kv = jnp.concatenate([dot(normed, w_k[...]), dot(normed, w_v[...])], axis=1)
-        qs_main[:, 0:q_cols] = q[0:n_main].astype(BF16)
-        qs_main[:, q_cols:cols] = kv[0:n_main].astype(BF16)
-        tail = jnp.concatenate([q[n_main:], kv[n_main:]], axis=1)
-        for g in range(n_rows):
-            for k in range(chunks):
-                at = g * 16 + k * n_tp
-                tail_f[at : at + n_tp, :] = tail[g * n_tp : (g + 1) * n_tp, cw * k : cw * k + cw]
-        qs_tail[...] = tail_f[...].astype(BF16)
-
-        def qsend(i, c):
-            for copy in q_copies(s, lax.rem(r + i, n_rows), r):
-                copy.start()
-            return c
-
-        lax.fori_loop(1, n_rows, qsend, 0)
-        for a_ref, b_ref, rows in (
-            (qs_main, qr_main, g_main), (qs_tail, qr_tail, 16), (ss_send, ss_recv, hs)
-        ):
-            at = pl.ds(pl.multiple_of(r * rows, rows), rows)
-            b_ref[s, at, :] = a_ref[at, :]
-
-        def qrecv(i, c):
-            for copy in q_copies(s, r, lax.rem(r + n_rows - i, n_rows)):
-                copy.wait_recv()
-            return c
-
-        lax.fori_loop(1, n_rows, qrecv, 0)
+        def nsend(i, c):
+            n_copy(s, lax.rem(r + i, n_rows), r).start()
+            return c
+
+        lax.fori_loop(1, n_rows, nsend, 0)
+        at = pl.ds(pl.multiple_of(r * hs, 8), hs)
+        ss_recv[s, at, :] = ss_send[at, :]
+
+        for p in range(chunks):
+            parts = []
+            for w_ref, first, width in (
+                (w_q, 0, q_cols), (w_k, q_cols, kv_cols), (w_v, q_cols + kv_cols, kv_cols)
+            ):
+                a_col = max(p * cw, first) - first
+                b_col = min((p + 1) * cw, first + width) - first
+                if a_col < b_col:
+                    parts.append(dot(normed, w_ref[:, a_col:b_col]))
+            part = parts[0] if len(parts) == 1 else jnp.concatenate(parts, axis=1)
+            for g in range(n_rows):
+                pos = (g % inner) * outer + g // inner
+                qs_main[p, pos * g_main : (pos + 1) * g_main, :] = part[
+                    g * g_main : (g + 1) * g_main
+                ].astype(BF16)
+                at = pos * 16 + p * n_tp
+                tail_f[at : at + n_tp, :] = part[n_main + g * n_tp : n_main + (g + 1) * n_tp]
+            if p == chunks - 1:
+                qs_tail[...] = tail_f[...].astype(BF16)
+            for q in (p,) if p < chunks - 1 else (p, chunks):
+                for i in range(1, inner):
+                    x_copy(s, q, lax.rem(lo + i, inner), lo).start()
+
+        for p in range(chunks + 1):
+            for i in range(1, inner):
+                x_copy(s, p, lo, lax.rem(lo + inner - i, inner)).wait_recv()
+            rows = outer * (g_main if p < chunks else 16)
+            mine = pl.ds(pl.multiple_of(lo * rows, 16), rows)
+            y = (qs_main[p, mine, :] if p < chunks else qs_tail[mine, :]).astype(F32)
+            for i in range(1, inner):
+                other = lax.rem(lo + i, inner)
+                y = y + (xr_main[s, p, other] if p < chunks else xr_tail[s, other]).astype(F32)
+            if p < chunks:
+                ys_main[p] = y.astype(BF16)
+            else:
+                ys_tail[...] = y.astype(BF16)
+            for i in range(1, outer):
+                z_copy(s, p, lax.rem(hi + i, outer), hi).start()
+            if p < chunks:
+                qr_main[s, p, hi] = ys_main[p, pl.ds(pl.multiple_of(hi * g_main, 16), g_main), :]
+            else:
+                qr_tail[s, hi] = ys_tail[pl.ds(pl.multiple_of(hi * 16, 16), 16), :]
+        for i in range(1, n_rows):
+            n_copy(s, r, lax.rem(r + n_rows - i, n_rows)).wait_recv()
+        for p in range(chunks + 1):
+            for i in range(1, outer):
+                z_copy(s, p, hi, lax.rem(hi + outer - i, outer)).wait_recv()
 
         inv = ss_recv[s, 0:hs, :]
-        tsum_v = qr_tail[s, 0:16, :].astype(F32)
+        tsum_v = qr_tail[s, 0].astype(F32)
+        for g in range(1, outer):
+            tsum_v = tsum_v + qr_tail[s, g].astype(F32)
         for g in range(1, n_rows):
             inv = inv + ss_recv[s, g * hs : (g + 1) * hs, :]
-            tsum_v = tsum_v + qr_tail[s, g * 16 : (g + 1) * 16, :].astype(F32)
         inv = lax.rsqrt(inv * (1.0 / dg) + EPS)
         tsum[...] = tsum_v
         for h in range(cols // HD):
-            at = slice(h * HD, (h + 1) * HD)
-            v = qr_main[s, 0:g_main, at].astype(F32)
-            for g in range(1, n_rows):
-                v = v + qr_main[s, g * g_main : (g + 1) * g_main, at].astype(F32)
+            k, off = (h * HD) // cw, (h * HD) % cw
+            v = qr_main[s, k, 0, :, off : off + HD].astype(F32)
+            for g in range(1, outer):
+                v = v + qr_main[s, k, g, :, off : off + HD].astype(F32)
             qf[h * hs : h * hs + g_main, :] = (v * inv[0:g_main]).astype(BF16).astype(F32)
-            k, off = (h * HD) // cw, (h * HD) % cw
             tv = tsum[k * n_tp : (k + 1) * n_tp, off : off + HD]
             qf[h * hs + g_main : h * hs + g_main + g_tail, :] = (
                 (tv * inv[g_main : g_main + g_tail]).astype(BF16).astype(F32)
@@ -337,21 +432,33 @@
         done = jnp.sum(back, axis=1, keepdims=True) > 0.0
         ctx_s[...] = jnp.where(done, delivered, ctx_s[...])
 
-        def drain_ag(i, c):
-            ag_copy(s, lax.rem(me + i, n_dev), me).wait_send()
-            return c
-
-        def drain_q(i, c):
-            for copy in q_copies(s, lax.rem(r + i, n_rows), r):
-                copy.wait_send()
+        def drain_rows(i, c):
+            to = lax.rem(r + i, n_rows)
+            ag_rows(s, to, r).wait_send()
+            n_copy(s, to, r).wait_send()
+            return c
+
+        def drain_own(i, c):
+            ag_own(s, lax.rem(t + i, n_tp), t).wait_send()
+            return c
+
+        def drain_forward(i, c):
+            for k in range(1, n_tp):
+                ag_forward(s, lax.rem(r + n_rows - i, n_rows), lax.rem(t + k, n_tp), t).wait_send()
             return c
 
         def drain_tp(i, c):
             tp_copy(s, lax.rem(t + i, n_tp), t).wait_send()
             return c
 
-        lax.fori_loop(1, n_dev, drain_ag, 0)
-        lax.fori_loop(1, n_rows, drain_q, 0)
+        lax.fori_loop(1, n_rows, drain_rows, 0)
+        lax.fori_loop(1, n_tp, drain_own, 0)
+        lax.fori_loop(1, n_rows, drain_forward, 0)
+        for p in range(chunks + 1):
+            for i in range(1, inner):
+                x_copy(s, p, lax.rem(lo + i, inner), lo).wait_send()
+            for i in range(1, outer):
+                z_copy(s, p, lax.rem(hi + i, outer), hi).wait_send()
         lax.fori_loop(1, n_tp, drain_tp, 0)
         return carry
 
@@ -375,6 +482,9 @@
     cols = q_cols + 2 * kv_cols
     hs = -(-slots // 8) * 8
     cache = key_cache.shape[1]
+    outer = min(4, n_rows)
+    inner = n_rows // outer
+    chunks = 16 // n_tp
     n_heads = q_cols // HD
     att_rows = slots * n_heads
     cw = cols * n_tp // 16
@@ -415,11 +525,15 @@
             pltpu.VMEM((16, 3 * dl // 8), BF16),
             pltpu.VMEM((n_steps, n_dev * 16, 3 * dl // 8), BF16),
             pltpu.VMEM((5 * n_dev, dl), BF16),
-            pltpu.VMEM((4 * n_dev, cols), BF16),
+            pltpu.VMEM((chunks, 4 * n_dev, cw), BF16),
             pltpu.VMEM((16 * n_rows, cw), F32),
             pltpu.VMEM((16 * n_rows, cw), BF16),
-            pltpu.VMEM((n_steps, 4 * n_dev, cols), BF16),
-            pltpu.VMEM((n_steps, 16 * n_rows, cw), BF16),
+            pltpu.VMEM((n_steps, chunks, inner, outer * 4 * n_tp, cw), BF16),
+            pltpu.VMEM((n_steps, inner, outer * 16, cw), BF16),
+            pltpu.VMEM((chunks, outer * 4 * n_tp, cw), BF16),
+            pltpu.VMEM((outer * 16, cw), BF16),
+            pltpu.VMEM((n_steps, chunks, outer, 4 * n_tp, cw), BF16),
+            pltpu.VMEM((n_steps, outer, 16, cw), BF16),
             pltpu.VMEM((n_rows * hs, 128), F32),
             pltpu.VMEM((n_steps, n_rows * hs, 128), F32),
             pltpu.VMEM((cols // HD * hs, HD), F32),
@@ -432,10 +546,15 @@
             pltpu.VMEM((n_tp * 8, dl), F32),
             pltpu.VMEM((n_steps, n_tp * 8, dl), F32),
             dma((len(weights),)),
-            dma((n_dev,)),
+            dma((n_rows,)),
+            dma((n_rows, n_tp)),
             dma((n_steps, n_dev)),
-            dma((3, n_rows)),
-            dma((n_steps, 3, n_rows)),
+            dma((chunks + 1, inner)),
+            dma((n_steps, chunks + 1, inner)),
+            dma((chunks + 1, outer)),
+            dma((n_steps, chunks + 1, outer)),
+            dma((n_rows,)),
+            dma((n_steps, n_rows)),
             dma((n_tp,)),
             dma((n_steps, n_tp)),
         ],

time: 180 us -> 152 us (0.84); the launches traced: 180 us -> 150 us
  Pallas kernels: 169 us -> 138 us
    pallas_call x1, Pallas kernels: 169 us -> 138 us  [on_device(): pl.pallas_call(functools.partial(kernel, n_rows, n_tp, n_steps), out_shap...]
where the time goes in v2:
time: 152 us; the launch traced here: 150 us
  Pallas kernels  138 us (91%)
  local copies, waits for them, and re-layouts  8.28 us (5%)
  other arithmetic  2.24 us (1%)
    pallas_call x1, Pallas kernels, on_device(): pl.pallas_call(functools.partial(kernel, n_rows, n_tp, n_steps), out_shap...  138 us

profile of v2, /device:TPU:11, one launch (start us, length us, event | category | flops | bytes accessed | tf_op | source)
XLA Modules:
  0.0 149.7 jit_solution(6989166709870978797)
XLA Ops:
  0.6 0.0 copy-start
  0.6 0.8 eq.44
  1.4 1.3 reshape.82.gg_ref
  2.7 0.8 broadcast_in_dim_reshape.3
  3.5 0.7 reduce_window_sum.11
  4.2 0.1 select_reduce_fusion
  4.3 0.1 broadcast_add_fusion
  4.4 0.1 add.58.idx_ref
  4.5 0.0 copy-start.1
  4.5 0.1 add.61
  4.6 0.0 copy-done
  4.7 1.2 gather_fusion
  5.9 0.5 and_select_fusion.len_ref
  6.4 0.1 fusion
  6.5 0.7 fusion.1.oh_ref
  7.2 0.6 pad_bitcast_fusion.pickt_ref
  7.8 0.1 copy.36
  7.9 0.6 pad.4.clone.pick_ref
  8.5 0.0 copy-done.1
  8.5 138.4 %shard_map.203 = (f32[8,1024]{1,0:T(8,128)}, bf16[8,1024]{1,0:T(8,128)(2,1)}) custom-call(s32[80]{0:T(128)} %copy-done.1, s32[80]{0:T(128)} %and_select_fusion.len_ref, bf16[8,1024]{1,0:T(8,128)(2,1)} %hidden_ref.1, bf16[8,1024]{1,0:T(8,128)(2,1)} %context_ref.1, bf16[32,256]{1,0:T(8,128)(2,1)} %fusion.1.oh_ref, f32[4,8,8]{2,1,0:T(8,128)} %pad.4.clone.pick_ref, ...), custom_call_target="tpu_custom_call" | custom-call | tf_op jit(solution)/shard_map/pallas_call | solution.py:510
  147.0 1.4 copy.35
  148.3 1.3 copy.38
  (9 shorter events, 0.1 us)
Async XLA Ops:
  0.6 4.0 %copy-start = (s32[32]{0:T(128)S(1)}, s32[32]{0:T(128)}, u32[]{:S(2)}) copy-start(s32[32]{0:T(128)} %param.24) | copy-start | bytes 388
  4.5 4.0 %copy-start.1 = (s32[80]{0:T(128)}, s32[80]{0:T(128)S(1)}, u32[]{:S(2)}) copy-start(s32[80]{0:T(128)S(1)} %add.58.idx_ref) | copy-start | bytes 964

commit v3 on v2

--- a/solution.py
+++ b/solution.py
@@ -23,7 +23,9 @@
 
 
 def slot_picker(finished):
-    ranked = jnp.cumsum(finished, axis=-1) - 1
+    place = jnp.arange(finished.shape[-1], dtype=jnp.int32)
+    before = (place[:, None] > place[None, :]).astype(jnp.int32)
+    ranked = jnp.sum(finished[..., None, :] * before, axis=-1)
     slot_ids = jnp.arange(CAP, dtype=jnp.int32)
     chosen = (finished[..., None, :] == 1) & (ranked[..., None, :] == slot_ids[:, None])
     return chosen.astype(jnp.int32)
@@ -46,7 +48,7 @@
 
 def kernel(
     n_rows, n_tp, n_steps,
-    idx_ref, len_ref, hidden_ref, context_ref, oh_ref, pick_ref, pickt_ref, unpack_ref,
+    idx_ref, len_ref, hidden_ref, context_ref, oh_ref, pick_ref, unpack_ref,
     gl_ref, og_ref, gg_ref,
     embed_hbm, w_in_hbm, w_out_hbm, w_vocab_hbm, w_up_hbm, w_q_hbm, w_k_hbm, w_v_hbm,
     kc_hbm, vc_hbm, w_mix_hbm,
@@ -91,7 +93,7 @@
             ]
         )
     ]
-    for c in loads:
+    for c in loads[:5]:
         c.start()
 
     barrier = pltpu.get_barrier_semaphore()
@@ -205,6 +207,8 @@
         def _():
             loads[1].wait()
             loads[2].wait()
+            for c in loads[5:]:
+                c.start()
 
         f = dot(a, w_in[...])
         f = (f / (1.0 + jnp.exp(-f))).astype(BF16)
@@ -376,7 +380,7 @@
                     pairs.append((tt, c, j, v))
         for p, (tt, c, j, v) in enumerate(pairs):
             row = idx_ref[s * n_slots + tt * CAP + c]
-            length = len_ref[s * n_slots + tt * CAP + c]
+            length = len_ref[row]
             q8 = qf[pl.ds(v * group * hs + j, group, stride=hs), :]
             nk = qf[pl.ds((n_heads + v) * hs + j, 1), :]
             keys = kc[row, :, v * HD : (v + 1) * HD]
@@ -427,9 +431,17 @@
         patch = tp_recv[s, 0:8, :]
         for g in range(1, n_tp):
             patch = patch + tp_recv[s, g * 8 : (g + 1) * 8, :]
-        back = pickt_ref[s]
-        delivered = dot(back.astype(BF16), patch.astype(BF16))
-        done = jnp.sum(back, axis=1, keepdims=True) > 0.0
+        back = pick_ref[s].astype(BF16)
+        to_rows = (((0,), (0,)), ((), ()))
+        delivered = lax.dot_general(
+            back, patch.astype(BF16), to_rows, preferred_element_type=F32
+        )
+        done = (
+            lax.dot_general(
+                back, jnp.ones((8, 128), BF16), to_rows, preferred_element_type=F32
+            )[:, 0:1]
+            > 0.0
+        )
         ctx_s[...] = jnp.where(done, delivered, ctx_s[...])
 
         def drain_rows(i, c):
@@ -495,10 +507,8 @@
     picker = slot_picker(finish.T.reshape(n_steps, n_tp, rows))
     local = jnp.sum(picker * jnp.arange(rows, dtype=jnp.int32), axis=-1)
     row_index = (local + jnp.arange(n_tp, dtype=jnp.int32)[:, None] * rows).reshape(-1)
-    lengths = jnp.take(cache_len, row_index, axis=0)
     mine = lax.dynamic_index_in_dim(picker, t, 1, keepdims=False).astype(F32)
     pick = jnp.pad(mine, ((0, 0), (0, 8 - CAP), (0, 0)))
-    pickt = pick.transpose(0, 2, 1)
 
     vm = pl.BlockSpec(memory_space=pltpu.VMEM)
     sm = pl.BlockSpec(memory_space=pltpu.SMEM)
@@ -513,7 +523,7 @@
             jax.ShapeDtypeStruct((rows, n_steps * vocab), F32),
             jax.ShapeDtypeStruct((rows, dl), BF16),
         ),
-        in_specs=[sm, sm] + [vm] * 9 + [anys] * len(weights),
+        in_specs=[sm, sm] + [vm] * 8 + [anys] * len(weights),
         out_specs=(vm, vm),
         scratch_shapes=[pltpu.VMEM(w.shape, w.dtype) for w in weights]
         + [
@@ -562,7 +572,7 @@
             collective_id=0, has_side_effects=True, vmem_limit_bytes=56 * 1024 * 1024
         ),
     )(
-        row_index, lengths, hidden, context, oh, pick, pickt,
+        row_index, cache_len, hidden, context, oh, pick,
         jnp.asarray(unpack_matrix(), BF16),
         gain_local.reshape(1, -1), output_norm_gain.reshape(1, -1), gain_global.reshape(1, -1),
         *weights,

time: 152 us -> 150 us (0.987)
  no operation moved by 1% of the time
where the time goes in v3:
time: 150 us; the launch traced here: 148 us
  Pallas kernels  139 us (93%)
  local copies, waits for them, and re-layouts  6.79 us (5%)
  other arithmetic  1.51 us (1%)
    pallas_call x1, Pallas kernels, on_device(): pl.pallas_call(functools.partial(kernel, n_rows, n_tp, n_steps), out_shap...  139 us

profile of v3, /device:TPU:11, one launch (start us, length us, event | category | flops | bytes accessed | tf_op | source)
XLA Modules:
  0.0 147.8 jit_solution(3760609915560487375)
XLA Ops:
  0.6 0.8 eq.44
  1.4 1.3 reshape.53.gg_ref
  2.7 0.8 broadcast_in_dim_reshape.4
  3.5 0.4 multiply_reduce_fusion
  3.8 0.4 select_reduce_fusion
  4.2 0.1 broadcast_add_fusion
  4.3 0.6 add.20.idx_ref
  5.0 0.6 pad.4.pick_ref
  5.6 0.7 fusion.1.oh_ref
  6.3 138.8 %shard_map.203 = (f32[8,1024]{1,0:T(8,128)}, bf16[8,1024]{1,0:T(8,128)(2,1)}) custom-call(s32[80]{0:T(128)} %add.20.idx_ref, s32[32]{0:T(128)} %len_ref.1, bf16[8,1024]{1,0:T(8,128)(2,1)} %hidden_ref.1, bf16[8,1024]{1,0:T(8,128)(2,1)} %context_ref.1, bf16[32,256]{1,0:T(8,128)(2,1)} %fusion.1.oh_ref, f32[4,8,8]{2,1,0:T(8,128)} %pad.4.pick_ref, ...), custom_call_target="tpu_custom_call" | custom-call | tf_op jit(solution)/shard_map/pallas_call | solution.py:520
  145.1 1.4 copy.30
  146.5 1.3 copy.32
  (8 shorter events, 0.1 us)
